TPU v7x, 128 devices: a whole 4x4x4 slice. The times are simulated.
128 devices in a mesh: dp: 16 (over z, y), expert: 8 (over x, core).
Axes of the slice: x: 4, y: 4, z: 4, core: 2. Of those that a mesh axis runs over, the one named last changes fastest.
Arguments:
- tokens: bfloat16 [16384, 1536], P(('dp', 'expert')), may hold values from -6 to 6
- segments: int32 [16384], P(('dp', 'expert')), may hold values from 0 to 2, as said below
- routes: int32 [16384, 8], P(('dp', 'expert')), may hold values from 0 to 15, all different within a row; in each aligned block of 128 rows (0 to 127, 128 to 255, ...) at most 96 rows name the same one
- gain_attn: bfloat16 [1536], P('dp'), may hold values from 0.099609375 to 1.8984375
- w_query: bfloat16 [1536, 1536], P('dp'), may hold values from -0.625 to 0.625
- w_key: bfloat16 [1536, 512], P('dp'), may hold values from -0.625 to 0.625
- w_value: bfloat16 [1536, 512], P('dp'), may hold values from -0.15625 to 0.15625
- w_out: bfloat16 [1536, 1536], P('dp'), may hold values from -6 to 6
- gain_moe: bfloat16 [1536], P('dp'), may hold values from 0.099609375 to 1.8984375
- w_router: bfloat16 [1536, 16], P('dp'), may hold values from -0.078125 to 0.078125
- expert_gate: bfloat16 [16, 1536, 512], P('expert'), may hold values from -0.15625 to 0.15625
- expert_up: bfloat16 [16, 1536, 512], P('expert'), may hold values from -0.15625 to 0.15625
- expert_down: bfloat16 [16, 512, 1536], P('expert'), may hold values from -6 to 6
- out_grad: bfloat16 [16384, 1536], P(('dp', 'expert')), may hold values from -6 to 6
Outputs:
- output: bfloat16 [16384, 1536], P(('dp', 'expert'))
- grad_tokens: float32 [16384, 1536], P(('dp', 'expert'))
- grad_gain_attn: float32 [1536], P('dp')
- grad_query: float32 [1536, 1536], P('dp')
- grad_key: float32 [1536, 512], P('dp')
- grad_value: float32 [1536, 512], P('dp')
- grad_out: float32 [1536, 1536], P('dp')
- grad_gain_moe: float32 [1536], P('dp')
- grad_router: float32 [1536, 16], P('dp')
- grad_gate: float32 [16, 1536, 512], P('expert')
- grad_up: float32 [16, 1536, 512], P('expert')
- grad_down: float32 [16, 512, 1536], P('expert')
Inputs may be any that keep to these rules, and one draw needn't show every extreme that they name: `segments`: within each sequence of 1024 tokens the id starts at 0 and never falls; every id from 0 to 2 occurs in every sequence. `routes`: each row names 8 different experts; among the rows of one device (aligned blocks of 128 rows) no expert is named more than 96 times, and in some block one is named exactly 96 times.
All inputs are finite; a program needn't handle non-finite values.
Results may differ from a plain program's by a relative error of at most 0.025.
Values may be sent and summed in bfloat16 or wider, within the bound.
No kernel may reach another device: no remote copies, remote signals or barrier semaphores. Data moves between devices by JAX's collectives and lax.ppermute only.
A program may use at most 256 MiB of HBM per device.

v0:
```python
import jax
import jax.numpy as jnp
from jax import lax
from jax.sharding import PartitionSpec as P

HEADS = 24
KV_HEADS = 8
HEAD_DIM = 64
TOP = 8
EXPERTS = 16


eps = 1e-06
residual_scale = 0.22
score_scale = 0.015625
rope_base = 10000.0
doc_slots = 3


def entering(value, axis, join, neutral):
    count, mine = (lax.axis_size(axis), lax.axis_index(axis))
    pieces = lax.all_gather(value, axis)
    so_far = jnp.full_like(value, 0) + jnp.asarray(neutral, value.dtype)

    def step(position, so_far):
        longer = join(so_far, pieces[position])
        return jnp.where(position < mine, longer, so_far)

    return lax.fori_loop(0, count - 1, step, so_far)


def inverse_rms(values):
    return lax.rsqrt(jnp.mean(values * values, axis=-1, keepdims=True) + eps)


def rotate(values, positions, direction):
    half_dim = values.shape[-1] // 2
    inv_freq = rope_base ** (-jnp.arange(half_dim, dtype=jnp.float32) * 2.0 / values.shape[-1])
    angles = positions.astype(jnp.float32)[:, None] * inv_freq[None, :]
    cosine = jnp.cos(angles)[:, None, :]
    sine_part = direction * jnp.sin(angles)[:, None, :]
    first_half = values[..., :half_dim]
    second_half = values[..., half_dim:]
    return jnp.concatenate(
        [
            first_half * cosine - second_half * sine_part,
            second_half * cosine + first_half * sine_part,
        ],
        axis=-1,
    )


def add_counts(earlier, later):
    return earlier + later


def per_device(
    tokens,
    segments,
    routes,
    gain_attn,
    w_query,
    w_key,
    w_value,
    w_out,
    gain_moe,
    w_router,
    expert_gate,
    expert_up,
    expert_down,
    out_grad,
):
    rows_here = tokens.shape[0]
    width = tokens.shape[1]
    seq_len = rows_here * lax.axis_size("expert")
    per_group = HEADS // KV_HEADS
    gain_one, query_w, key_w, value_w, out_w, gain_two, router_w = (
        lax.all_gather(gain_attn, "dp", axis=0, tiled=True),
        lax.all_gather(w_query, "dp", axis=0, tiled=True),
        lax.all_gather(w_key, "dp", axis=0, tiled=True),
        lax.all_gather(w_value, "dp", axis=0, tiled=True),
        lax.all_gather(w_out, "dp", axis=0, tiled=True),
        lax.all_gather(gain_moe, "dp", axis=0, tiled=True),
        lax.all_gather(w_router, "dp", axis=0, tiled=True),
    )
    doc_hot = (segments[:, None] == jnp.arange(doc_slots, dtype=jnp.int32)[None, :]).astype(
        jnp.int32
    )
    before = entering(
        jnp.sum(doc_hot, axis=0), "expert", add_counts, jnp.zeros((doc_slots,), jnp.int32)
    )
    local_rank = jnp.cumsum(doc_hot, axis=0) - doc_hot
    positions = jnp.sum(doc_hot * (local_rank + before[None, :]), axis=1)
    inputs = tokens.astype(jnp.float32)
    scale_one = inverse_rms(inputs)
    gain_one_f = gain_one.astype(jnp.float32)
    normed = (inputs * scale_one * gain_one_f).astype(jnp.bfloat16)
    queries = jnp.dot(normed, query_w, preferred_element_type=jnp.float32)
    key_proj = jnp.dot(normed, key_w, preferred_element_type=jnp.float32)
    value_proj = jnp.dot(normed, value_w, preferred_element_type=jnp.float32)
    query_turned = rotate(queries.reshape(rows_here, HEADS, HEAD_DIM), positions, 1.0).astype(
        jnp.bfloat16
    )
    key_turned = (
        rotate(key_proj.reshape(rows_here, KV_HEADS, HEAD_DIM), positions, 1.0)
        .astype(jnp.bfloat16)
        .reshape(rows_here, KV_HEADS * HEAD_DIM)
    )
    value_low = value_proj.astype(jnp.bfloat16)
    key_all, value_all, seg_all = (
        lax.all_gather(key_turned, "expert", axis=0, tiled=True),
        lax.all_gather(value_low, "expert", axis=0, tiled=True),
        lax.all_gather(segments.astype(jnp.bfloat16), "expert", axis=0, tiled=True),
    )
    query_four = query_turned.reshape(rows_here, KV_HEADS, per_group, HEAD_DIM)
    key_three = key_all.reshape(seq_len, KV_HEADS, HEAD_DIM)
    value_three = value_all.reshape(seq_len, KV_HEADS, HEAD_DIM)
    query_place = lax.axis_index("expert") * rows_here + jnp.arange(rows_here, dtype=jnp.int32)
    allowed = (segments[:, None] == seg_all.astype(jnp.int32)[None, :]) & (
        query_place[:, None] >= jnp.arange(seq_len, dtype=jnp.int32)[None, :]
    )

    def masked_scores():
        raw = jnp.einsum(
            "qgrd,kgd->grqk", query_four, key_three, preferred_element_type=jnp.float32
        )
        return jnp.where(allowed[None, None], raw * score_scale, -1e30)

    scores = masked_scores()
    maximum = jnp.max(scores, axis=-1, keepdims=True)
    exponent = jnp.exp(scores - maximum)
    denom_sum = jnp.sum(exponent, axis=-1, keepdims=True)
    log_total = maximum + jnp.log(denom_sum)
    attn_probs = (exponent / denom_sum).astype(jnp.bfloat16)
    mixed = (
        jnp.einsum("grqk,kgd->qgrd", attn_probs, value_three, preferred_element_type=jnp.float32)
        .reshape(rows_here, HEADS * HEAD_DIM)
        .astype(jnp.bfloat16)
    )
    hidden = inputs + residual_scale * jnp.dot(mixed, out_w, preferred_element_type=jnp.float32)
    scale_two = inverse_rms(hidden)
    gain_two_f = gain_two.astype(jnp.float32)
    second = (hidden * scale_two * gain_two_f).astype(jnp.bfloat16)
    logits = jnp.dot(second, router_w, preferred_element_type=jnp.float32)
    gate_probs = jax.nn.softmax(jnp.take_along_axis(logits, routes, axis=1), axis=1)
    pair_count = rows_here * TOP
    capacity = pair_count * 3 // (2 * EXPERTS)
    flat_routes = routes.reshape(pair_count)
    pair_hot = (flat_routes[:, None] == jnp.arange(EXPERTS, dtype=jnp.int32)[None, :]).astype(
        jnp.int32
    )
    slot_of = jnp.sum((jnp.cumsum(pair_hot, axis=0) - pair_hot) * pair_hot, axis=1)
    slot_table = (
        jnp.full((EXPERTS, capacity), pair_count, jnp.int32)
        .at[flat_routes, slot_of]
        .set(jnp.arange(pair_count, dtype=jnp.int32))
    )
    second_pad = jnp.concatenate([second, jnp.zeros((1, width), jnp.bfloat16)], axis=0)
    received = lax.all_to_all(
        second_pad[slot_table // TOP], "expert", split_axis=0, concat_axis=1, tiled=True
    )
    gate_pre = jnp.einsum("ecd,edf->ecf", received, expert_gate, preferred_element_type=jnp.float32)
    up_pre = jnp.einsum("ecd,edf->ecf", received, expert_up, preferred_element_type=jnp.float32)
    sigmoid_gate = jax.nn.sigmoid(gate_pre)
    silu_gate = gate_pre * sigmoid_gate
    hidden_act = (silu_gate * up_pre).astype(jnp.bfloat16)
    produced = jnp.einsum(
        "ecf,efd->ecd", hidden_act, expert_down, preferred_element_type=jnp.float32
    ).astype(jnp.bfloat16)
    returned = lax.all_to_all(produced, "expert", split_axis=1, concat_axis=0, tiled=True)
    pair_out = returned[flat_routes, slot_of].reshape(rows_here, TOP, width)
    combined = jnp.sum(gate_probs[:, :, None] * pair_out, axis=1)
    output = (hidden + residual_scale * combined).astype(jnp.bfloat16)
    grad_final = out_grad.astype(jnp.float32)
    grad_moe = residual_scale * grad_final
    grad_gates = jnp.sum(grad_moe[:, None, :] * pair_out, axis=2)
    grad_pair = (
        (gate_probs[:, :, None] * grad_moe[:, None, :])
        .astype(jnp.bfloat16)
        .reshape(pair_count, width)
    )
    grad_pad = jnp.concatenate([grad_pair, jnp.zeros((1, width), jnp.bfloat16)], axis=0)
    grad_recv = lax.all_to_all(
        grad_pad[slot_table], "expert", split_axis=0, concat_axis=1, tiled=True
    )
    grad_act = jnp.einsum(
        "ecd,efd->ecf", grad_recv, expert_down, preferred_element_type=jnp.float32
    )
    grad_w_down = jnp.einsum(
        "ecf,ecd->efd", hidden_act, grad_recv, preferred_element_type=jnp.float32
    )
    grad_gate_pre = (
        grad_act * up_pre * sigmoid_gate * (1.0 + gate_pre * (1.0 - sigmoid_gate))
    ).astype(jnp.bfloat16)
    grad_up_pre = (grad_act * silu_gate).astype(jnp.bfloat16)
    grad_w_gate = jnp.einsum(
        "ecd,ecf->edf", received, grad_gate_pre, preferred_element_type=jnp.float32
    )
    grad_w_up = jnp.einsum(
        "ecd,ecf->edf", received, grad_up_pre, preferred_element_type=jnp.float32
    )
    grad_in_rows = jnp.einsum(
        "ecf,edf->ecd", grad_gate_pre, expert_gate, preferred_element_type=jnp.float32
    ) + jnp.einsum("ecf,edf->ecd", grad_up_pre, expert_up, preferred_element_type=jnp.float32)
    grad_back = lax.all_to_all(
        grad_in_rows.astype(jnp.bfloat16), "expert", split_axis=1, concat_axis=0, tiled=True
    ).astype(grad_in_rows.dtype)
    grad_w_gate, grad_w_up, grad_w_down = (
        lax.psum(grad_w_gate.astype(jnp.bfloat16), "dp").astype(jnp.float32),
        lax.psum(grad_w_up.astype(jnp.bfloat16), "dp").astype(jnp.float32),
        lax.psum(grad_w_down.astype(jnp.bfloat16), "dp").astype(jnp.float32),
    )
    grad_second = jnp.sum(grad_back[flat_routes, slot_of].reshape(rows_here, TOP, width), axis=1)
    highest = lax.Precision.HIGHEST
    grad_chosen = gate_probs * (
        grad_gates - jnp.sum(gate_probs * grad_gates, axis=1, keepdims=True)
    )
    route_hot = pair_hot.reshape(rows_here, TOP, EXPERTS).astype(jnp.float32)
    grad_logits = jnp.einsum("tk,tke->te", grad_chosen, route_hot, precision=highest)
    second_f = second.astype(jnp.float32)
    grad_router_w = jnp.einsum("td,te->de", second_f, grad_logits, precision=highest)
    grad_second = grad_second + jnp.einsum(
        "te,de->td", grad_logits, router_w.astype(jnp.float32), precision=highest
    )
    scaled_two = grad_second * gain_two_f
    grad_gain_two = jnp.sum(grad_second * hidden * scale_two, axis=0)
    grad_hidden = (
        grad_final
        + scale_two * scaled_two
        - hidden * scale_two**3 * jnp.mean(hidden * scaled_two, axis=-1, keepdims=True)
    )
    grad_branch = (residual_scale * grad_hidden).astype(jnp.bfloat16)
    grad_w_out = jnp.einsum("te,td->ed", mixed, grad_branch, preferred_element_type=jnp.float32)
    grad_mixed = jnp.einsum(
        "td,ed->te", grad_branch, out_w, preferred_element_type=jnp.float32
    ).astype(jnp.bfloat16)
    grad_four = grad_mixed.reshape(rows_here, KV_HEADS, per_group, HEAD_DIM)
    again = jnp.exp(masked_scores() - log_total)
    grad_probs = jnp.einsum(
        "qgrd,kgd->grqk", grad_four, value_three, preferred_element_type=jnp.float32
    )
    delta_sum = jnp.sum(again * grad_probs, axis=-1, keepdims=True)
    grad_raw = (again * (grad_probs - delta_sum) * score_scale).astype(jnp.bfloat16)
    grad_query_turned = jnp.einsum(
        "grqk,kgd->qgrd", grad_raw, key_three, preferred_element_type=jnp.float32
    ).reshape(rows_here, HEADS, HEAD_DIM)
    grad_key_all = jnp.einsum(
        "grqk,qgrd->kgd", grad_raw, query_four, preferred_element_type=jnp.float32
    ).reshape(seq_len, KV_HEADS * HEAD_DIM)
    grad_value_all = jnp.einsum(
        "grqk,qgrd->kgd", again.astype(jnp.bfloat16), grad_four, preferred_element_type=jnp.float32
    ).reshape(seq_len, KV_HEADS * HEAD_DIM)
    grad_key_turned, grad_value_sum = (
        lax.psum_scatter(
            grad_key_all.astype(jnp.bfloat16), "expert", scatter_dimension=0, tiled=True
        ).astype(jnp.float32),
        lax.psum_scatter(
            grad_value_all.astype(jnp.bfloat16), "expert", scatter_dimension=0, tiled=True
        ).astype(jnp.float32),
    )
    grad_queries = (
        rotate(grad_query_turned, positions, -1.0)
        .astype(jnp.bfloat16)
        .reshape(rows_here, HEADS * HEAD_DIM)
    )
    grad_keys = (
        rotate(grad_key_turned.reshape(rows_here, KV_HEADS, HEAD_DIM), positions, -1.0)
        .astype(jnp.bfloat16)
        .reshape(rows_here, KV_HEADS * HEAD_DIM)
    )
    grad_values = grad_value_sum.astype(jnp.bfloat16)
    grad_w_query = jnp.einsum("td,te->de", normed, grad_queries, preferred_element_type=jnp.float32)
    grad_w_key = jnp.einsum("td,te->de", normed, grad_keys, preferred_element_type=jnp.float32)
    grad_w_value = jnp.einsum("td,te->de", normed, grad_values, preferred_element_type=jnp.float32)
    grad_normed = jnp.einsum("te,de->td", grad_queries, query_w, preferred_element_type=jnp.float32)
    grad_normed = grad_normed + jnp.einsum(
        "te,de->td", grad_keys, key_w, preferred_element_type=jnp.float32
    )
    grad_normed = grad_normed + jnp.einsum(
        "te,de->td", grad_values, value_w, preferred_element_type=jnp.float32
    )
    scaled_one = grad_normed * gain_one_f
    grad_gain_one = jnp.sum(grad_normed * inputs * scale_one, axis=0)
    grad_inputs = (
        grad_hidden
        + scale_one * scaled_one
        - inputs * scale_one**3 * jnp.mean(inputs * scaled_one, axis=-1, keepdims=True)
    )
    shares = (
        lax.psum_scatter(
            grad_gain_one.astype(jnp.bfloat16), "dp", scatter_dimension=0, tiled=True
        ).astype(jnp.float32),
        lax.psum_scatter(
            grad_w_query.astype(jnp.bfloat16), "dp", scatter_dimension=0, tiled=True
        ).astype(jnp.float32),
        lax.psum_scatter(
            grad_w_key.astype(jnp.bfloat16), "dp", scatter_dimension=0, tiled=True
        ).astype(jnp.float32),
        lax.psum_scatter(
            grad_w_value.astype(jnp.bfloat16), "dp", scatter_dimension=0, tiled=True
        ).astype(jnp.float32),
        lax.psum_scatter(
            grad_w_out.astype(jnp.bfloat16), "dp", scatter_dimension=0, tiled=True
        ).astype(jnp.float32),
        lax.psum_scatter(
            grad_gain_two.astype(jnp.bfloat16), "dp", scatter_dimension=0, tiled=True
        ).astype(jnp.float32),
        lax.psum_scatter(
            grad_router_w.astype(jnp.bfloat16), "dp", scatter_dimension=0, tiled=True
        ).astype(jnp.float32),
    )
    summed = (
        lax.psum(shares[0].astype(jnp.bfloat16), "expert").astype(jnp.float32),
        lax.psum(shares[1].astype(jnp.bfloat16), "expert").astype(jnp.float32),
        lax.psum(shares[2].astype(jnp.bfloat16), "expert").astype(jnp.float32),
        lax.psum(shares[3].astype(jnp.bfloat16), "expert").astype(jnp.float32),
        lax.psum(shares[4].astype(jnp.bfloat16), "expert").astype(jnp.float32),
        lax.psum(shares[5].astype(jnp.bfloat16), "expert").astype(jnp.float32),
        lax.psum(shares[6].astype(jnp.bfloat16), "expert").astype(jnp.float32),
    )
    sum_gain_one, sum_query, sum_key, sum_value, sum_out, sum_gain_two, sum_router = summed
    return (
        output,
        grad_inputs,
        sum_gain_one,
        sum_query,
        sum_key,
        sum_value,
        sum_out,
        sum_gain_two,
        sum_router,
        grad_w_gate,
        grad_w_up,
        grad_w_down,
    )


def solution(mesh):
    placed = (
        P(("dp", "expert"), None),
        P(("dp", "expert")),
        P(("dp", "expert"), None),
        P("dp"),
        P("dp", None),
        P("dp", None),
        P("dp", None),
        P("dp", None),
        P("dp"),
        P("dp", None),
        P("expert", None, None),
        P("expert", None, None),
        P("expert", None, None),
        P(("dp", "expert"), None),
    )
    return jax.shard_map(
        per_device,
        mesh=mesh,
        in_specs=placed,
        out_specs=(
            P(("dp", "expert"), None),
            P(("dp", "expert"), None),
            P("dp"),
            P("dp", None),
            P("dp", None),
            P("dp", None),
            P("dp", None),
            P("dp"),
            P("dp", None),
            P("expert", None, None),
            P("expert", None, None),
            P("expert", None, None),
        ),
        check_vma=False,
    )
```

profile of v0, /device:TPU:1, one launch (start us, length us, event | category | flops | bytes accessed | tf_op | source)
XLA Modules:
  0.0 1319.4 jit_solution(9778113286854868243)
XLA Ops:
  12.4 36.7 %all-reduce.8 = (bf16[1536]{0:T(1024)(128)(2,1)S(1)}, bf16[1536]{0:T(1024)(128)(2,1)}) all-reduce(bf16[1536]{0:T(1024)(128)(2,1)S(1)} %dynamic-update-slice, bf16[1536]{0:T(1024)(128)(2,1)S(1)} %dynamic-update-slice.2), channel_id=1, replica_groups=mesh['dp'=16,'expert'=8] {'dp'}, use_global_device_ids=true, to_apply=%add.2 | all-reduce | flops 3072 | bytes 12288
  162.0 22.1 %all-gather.18.cloned.1.call-done = bf16[1536,1536]{1,0:T(8,128)(2,1)} async-done(((bf16[96,1536]{1,0:T(8,128)(2,1)}), bf16[1536,1536]{1,0:T(8,128)(2,1)}) %all-gather.18.cloned.1.call-update) | async-done | bytes 4718608 | tf_op jit(solution)/shard_map/all_gather | solution.py:79
  189.3 20.2 %all-gather.16.cloned.1.call-done = bf16[1024,512]{0,1:T(8,128)(2,1)} async-done(((bf16[128,512]{0,1:T(8,128)(2,1)}), bf16[1024,512]{0,1:T(8,128)(2,1)}) %all-gather.16.cloned.1.call-update) | async-done | bytes 1048592 | tf_op jit(solution)/shard_map/all_gather | solution.py:111
  221.7 44.5 %all-gather.20.cloned.1.call-done = bf16[1536,1536]{1,0:T(8,128)(2,1)} async-done(((bf16[96,1536]{1,0:T(8,128)(2,1)}), bf16[1536,1536]{1,0:T(8,128)(2,1)}) %all-gather.20.cloned.1.call-update) | async-done | bytes 4718608 | tf_op jit(solution)/shard_map/all_gather | solution.py:82
  288.3 19.8 %all-gather.2 = bf16[16,96,16]{1,2,0:T(8,128)(2,1)S(1)} all-gather(bf16[1,96,16]{1,2,0:T(8,128)(2,1)S(1)} %bitcast.260), channel_id=1, replica_groups=mesh['dp'=16,'expert'=8] {'dp'}, dimensions={0}, use_global_device_ids=true | all-gather | bytes 52224 | tf_op jit(solution)/shard_map/all_gather | solution.py:84
  337.3 12.8 gather_fusion.2
  370.6 42.7 %all-to-all-done.2 = bf16[16,96,1536]{2,1,0:T(8,128)(2,1)} async-done(((bf16[16,96,1536]{2,1,0:T(8,128)(2,1)}), bf16[16,96,1536]{2,1,0:T(8,128)(2,1)}, u32[]{:S(2)}, u32[]{:S(2)}) %all-to-all-start.2) | async-done | bytes 4718624 | tf_op jit(solution)/shard_map/all_to_all | solution.py:183
  464.1 39.6 %all-to-all-done.3 = bf16[2,768,1536]{2,0,1:T(2,128)(2,1)} async-done(((bf16[2,768,1536]{2,0,1:T(2,128)(2,1)}), bf16[2,768,1536]{2,0,1:T(2,128)(2,1)}, u32[]{:S(2)}, u32[]{:S(2)}) %all-to-all-start.3) | async-done | bytes 4718624 | tf_op jit(solution)/shard_map/all_to_all | solution.py:205
  517.3 22.9 %gather_fusion.3 = f32[1024,1536]{1,0:T(8,128)} fusion(f32[16,96,1536]{2,1,0:T(8,128)} %bitcast.217, s32[1024]{0:T(1024)S(1)} %bitcast.218), kind=kCustom, calls=%fused_computation.3 | custom fusion | bytes 12591104 | tf_op jit(solution)/shard_map/gather | solution.py:213
  545.4 18.3 %all-to-all-done.1 = bf16[2,768,1536]{2,0,1:T(2,128)(2,1)} async-done(((bf16[2,768,1536]{2,0,1:T(2,128)(2,1)}), bf16[2,768,1536]{2,0,1:T(2,128)(2,1)}, u32[]{:S(2)}, u32[]{:S(2)}) %all-to-all-start.1) | async-done | bytes 4718624 | tf_op jit(solution)/shard_map/all_to_all | solution.py:170
  569.1 17.8 %gather_fusion.1 = bf16[1024,1536]{1,0:T(8,128)(2,1)S(1)} fusion(bf16[16,96,1536]{2,1,0:T(8,128)(2,1)} %bitcast.220, s32[1024]{0:T(1024)S(1)} %bitcast.219), kind=kCustom, calls=%fused_computation.1 | custom fusion | bytes 6299648 | tf_op jit(solution)/shard_map/gather | solution.py:171
  610.2 23.3 %bitcast_convert_fusion.1 = bf16[8,64,1024]{2,1,0:T(8,128)(2,1)S(1)} fusion(f32[8,1024,128,3]{2,1,3,0:T(8,128)} %fusion.81, f32[8,3,128]{2,1,0:T(4,128)S(1)} %copy-done.44, f32[8,1024,128,3]{2,1,3,0:T(8,128)} %copy-done.2, pred[128,1024]{0,1:T(8,128)(4,1)S(1)} %copy-done.20, bf16[128,8,3,32]{0,3,2,1:T(8,128)(2,1)S(1)} %bitcast.251, ...), kind=kOutput, calls=%fused_computation.56 | convolution fusion | flops 438571008 | bytes 26750976 | tf_op jit(solution)/shard_map/grqk,qgrd->kgd/dot_general | solution.py:247
  645.3 15.5 %reduce-scatter.22.cloned.1.call-done = bf16[128,512]{1,0:T(8,128)(2,1)} async-done(((bf16[1024,512]{1,0:T(8,128)(2,1)}), bf16[128,512]{1,0:T(8,128)(2,1)}) %reduce-scatter.22.cloned.1.call-update) | async-done | bytes 131088
  663.9 30.6 %reduce-scatter.24.cloned.1.call-done = bf16[128,512]{1,0:T(8,128)(2,1)} async-done(((bf16[1024,512]{1,0:T(8,128)(2,1)}), bf16[128,512]{1,0:T(8,128)(2,1)}) %reduce-scatter.24.cloned.1.call-update) | async-done | bytes 131088
  697.3 24.2 %fusion.18 = f32[8,64,3,128]{3,1,2,0:T(8,128)} fusion(bf16[1024,8,64,1]{0,2,3,1:T(8,128)(2,1)S(1)} %bitcast.246, f32[8,1024,128,3]{2,1,3,0:T(8,128)} %fusion.81, f32[8,3,128]{2,1,0:T(4,128)S(1)} %copy-done.44, f32[8,1024,128,3]{2,1,3,0:T(8,128)} %copy-done.2, pred[128,1024]{0,1:T(8,128)(4,1)S(1)} %copy-done.20), kind=kOutput, calls=%fused_computation.52 | convolution fusion | flops 437260288 | bytes 27144192 | tf_op jit(solution)/shard_map/grqk,kgd->qgrd/dot_general | solution.py:244
  756.0 14.7 %reduce-scatter.26.cloned.1.call-done = bf16[96,16]{1,0:T(8,128)(2,1)} async-done(((bf16[1536,16]{1,0:T(8,128)(2,1)}), bf16[96,16]{1,0:T(8,128)(2,1)}) %reduce-scatter.26.cloned.1.call-update) | async-done | bytes 3088
  775.6 31.5 %all-reduce.7 = (bf16[1536]{0:T(1024)(128)(2,1)S(1)}, bf16[1536]{0:T(1024)(128)(2,1)S(1)}) all-reduce(bf16[1536]{0:T(1024)(128)(2,1)S(1)} %get-tuple-element.111, bf16[1536]{0:T(1024)(128)(2,1)S(1)} %copy-done.43), channel_id=5, replica_groups=mesh['dp'=16,'expert'=8] {'dp'}, use_global_device_ids=true, to_apply=%region_25.26.clone | all-reduce | flops 3072 | bytes 12288
  807.3 21.7 %all-reduce.10 = (bf16[96]{0:T(256)(128)(2,1)S(1)}, bf16[96]{0:T(256)(128)(2,1)S(1)}, bf16[96,16]{0,1:T(8,128)(2,1)S(1)}) all-reduce(bf16[96]{0:T(256)(128)(2,1)S(1)} %dynamic-slice.4, bf16[96]{0:T(256)(128)(2,1)S(1)} %dynamic-slice.6, bf16[96,16]{0,1:T(8,128)(2,1)S(1)} %copy.183), channel_id=1, replica_groups=mesh['dp'=16,'expert'=8] {'expert'}, use_global_device_ids=true, to_apply=%region_26.27 | all-reduce | flops 1728 | bytes 6912 | tf_op jit(solution)/shard_map/psum | solution.py:313
  830.6 16.6 %reduce-scatter.16.cloned.1.call-done = bf16[96,512]{1,0:T(8,128)(2,1)} async-done(((bf16[1536,512]{1,0:T(8,128)(2,1)}), bf16[96,512]{1,0:T(8,128)(2,1)}) %reduce-scatter.16.cloned.1.call-update) | async-done | bytes 98320 | tf_op jit(solution)/shard_map/reduce_scatter | solution.py:296
  847.2 76.5 %reduce-scatter.18.cloned.1.call-done = bf16[96,512]{1,0:T(8,128)(2,1)} async-done(((bf16[1536,512]{1,0:T(8,128)(2,1)}), bf16[96,512]{1,0:T(8,128)(2,1)}) %reduce-scatter.18.cloned.1.call-update) | async-done | bytes 98320 | tf_op jit(solution)/shard_map/reduce_scatter | solution.py:299
  923.7 81.7 %reduce-scatter.14.cloned.1.call-done = bf16[96,1536]{1,0:T(8,128)(2,1)} async-done(((bf16[1536,1536]{1,0:T(8,128)(2,1)}), bf16[96,1536]{1,0:T(8,128)(2,1)}) %reduce-scatter.14.cloned.1.call-update) | async-done | bytes 294928 | tf_op jit(solution)/shard_map/reduce_scatter | solution.py:293
  1005.5 82.1 %reduce-scatter.20.cloned.1.call-done = bf16[96,1536]{1,0:T(8,128)(2,1)} async-done(((bf16[1536,1536]{1,0:T(8,128)(2,1)}), bf16[96,1536]{1,0:T(8,128)(2,1)}) %reduce-scatter.20.cloned.1.call-update) | async-done | bytes 294928 | tf_op jit(solution)/shard_map/reduce_scatter | solution.py:302
  1088.7 155.5 %all-reduce.15.cloned.1.call-done = (bf16[2,1536,512]{2,1,0:T(8,128)(2,1)}, bf16[2,1536,512]{2,1,0:T(8,128)(2,1)}, bf16[2,512,1536]{2,1,0:T(8,128)(2,1)}) async-done(((bf16[2,1536,512]{2,1,0:T(8,128)(2,1)}, bf16[2,1536,512]{2,1,0:T(8,128)(2,1)}, bf16[2,512,1536]{2,1,0:T(8,128)(2,1)}), (bf16[2,1536,512]{2,1,0:T(8,128)(2,1)}, bf16[2,1536,512]{2,1,0:T(8,128)(2,1)}, ...) | async-done | bytes 9437200 | tf_op jit(solution)/shard_map/psum | solution.py:209
  1257.1 48.8 %all-reduce.17.cloned.1.call-done = (bf16[96,1536]{1,0:T(8,128)(2,1)}, bf16[96,512]{1,0:T(8,128)(2,1)}, bf16[96,512]{1,0:T(8,128)(2,1)}, bf16[96,1536]{1,0:T(8,128)(2,1)}) async-done(((bf16[96,1536]{1,0:T(8,128)(2,1)}, bf16[96,512]{1,0:T(8,128)(2,1)}, bf16[96,512]{1,0:T(8,128)(2,1)}, bf16[96,1536]{1,0:T(8,128)(2,1)}), (bf16[96,1536]{1,0:T(8,128)(2,1)}, bf16[96,512]{1,0:T(8,128)(2,1)}, ...) | async-done | bytes 786448 | tf_op jit(solution)/shard_map/psum | solution.py:314
  (299 shorter events, 391.0 us)
Async XLA Ops:
  7.2 408.9 %copy-start = (bf16[2,512,1536]{2,1,0:T(8,128)(2,1)S(1)}, bf16[2,512,1536]{2,1,0:T(8,128)(2,1)}, u32[]{:S(2)}) copy-start(bf16[2,512,1536]{2,1,0:T(8,128)(2,1)} %param.28) | copy-start | bytes 9437188
  7.2 49.4 %all-gather.10.cloned.1.call-start = ((), (), s32[]{:S(2)}) async-start(), calls=%async_computation.11 | async-start | bytes 1671168 | tf_op jit(solution)/shard_map/all_gather | solution.py:81
  7.9 94.2 %all-gather.14.cloned.1.call-start = ((), (), s32[]{:S(2)}) async-start(), calls=%async_computation.13 | async-start | bytes 1671168 | tf_op jit(solution)/shard_map/all_gather | solution.py:80
  8.7 151.0 %all-gather.12.cloned.1.call-start = ((), (), s32[]{:S(2)}) async-start(), calls=%async_computation.12 | async-start | bytes 1179648 | tf_op jit(solution)/shard_map/all_gather | solution.py:112
  49.2 134.9 %copy-start.22 = (f32[1536]{0:T(1024)}, f32[1536]{0:T(1024)S(1)}, u32[]{:S(2)}) copy-start(f32[1536]{0:T(1024)S(1)} %convert_element_type.237) | copy-start | bytes 18436
  50.9 133.1 %copy-start.40 = (f32[128]{0:T(128)}, f32[128]{0:T(128)S(1)}, u32[]{:S(2)}) copy-start(f32[128]{0:T(128)S(1)} %get-tuple-element.159) | copy-start | bytes 1540
  56.6 127.4 %copy-start.3 = (bf16[128,1536]{1,0:T(8,128)(2,1)S(1)}, bf16[128,1536]{1,0:T(8,128)(2,1)}, u32[]{:S(2)}) copy-start(bf16[128,1536]{1,0:T(8,128)(2,1)} %param.16) | copy-start | bytes 1179652
  59.3 124.8 %all-gather.18.cloned.1.call-start = ((), (), s32[]{:S(2)}) async-start(), calls=%async_computation.15 | async-start | bytes 5013504 | tf_op jit(solution)/shard_map/all_gather | solution.py:79
  59.9 149.6 %all-gather.16.cloned.1.call-start = ((), (), s32[]{:S(2)}) async-start(), calls=%async_computation.14 | async-start | bytes 1179648 | tf_op jit(solution)/shard_map/all_gather | solution.py:111
  105.9 160.3 %all-gather.20.cloned.1.call-start = ((), (), s32[]{:S(2)}) async-start(), calls=%async_computation.16 | async-start | bytes 5013504 | tf_op jit(solution)/shard_map/all_gather | solution.py:82
  283.0 67.1 %all-to-all-start = ((bf16[16,96,1536]{2,1,0:T(8,128)(2,1)}), bf16[16,96,1536]{2,1,0:T(8,128)(2,1)}, u32[]{:S(2)}, u32[]{:S(2)}) async-start(bf16[16,96,1536]{2,1,0:T(8,128)(2,1)} %bitcast.221), calls=%async_computation | async-start | bytes 9437184 | tf_op jit(solution)/shard_map/all_to_all | solution.py:159
  350.1 63.1 %all-to-all-start.2 = ((bf16[16,96,1536]{2,1,0:T(8,128)(2,1)}), bf16[16,96,1536]{2,1,0:T(8,128)(2,1)}, u32[]{:S(2)}, u32[]{:S(2)}) async-start(bf16[16,96,1536]{2,1,0:T(8,128)(2,1)} %bitcast.222), calls=%async_computation.2 | async-start | bytes 9437184 | tf_op jit(solution)/shard_map/all_to_all | solution.py:183
  443.8 59.9 %all-to-all-start.3 = ((bf16[2,768,1536]{2,0,1:T(2,128)(2,1)}), bf16[2,768,1536]{2,0,1:T(2,128)(2,1)}, u32[]{:S(2)}, u32[]{:S(2)}) async-start(bf16[2,768,1536]{2,0,1:T(2,128)(2,1)} %copy.151), calls=%async_computation.3 | async-start | bytes 9437184 | tf_op jit(solution)/shard_map/all_to_all | solution.py:205
  503.7 59.9 %all-to-all-start.1 = ((bf16[2,768,1536]{2,0,1:T(2,128)(2,1)}), bf16[2,768,1536]{2,0,1:T(2,128)(2,1)}, u32[]{:S(2)}, u32[]{:S(2)}) async-start(bf16[2,768,1536]{2,0,1:T(2,128)(2,1)} %copy.147), calls=%async_computation.1 | async-start | bytes 9437184 | tf_op jit(solution)/shard_map/all_to_all | solution.py:170
  509.1 151.7 %reduce-scatter.22.cloned.1.call-start = ((), (), s32[]{:S(2)}) async-start(), calls=%async_computation.21 | async-start | bytes 1179648
  634.9 59.6 %reduce-scatter.24.cloned.1.call-start = ((), (), s32[]{:S(2)}) async-start(), calls=%async_computation.22 | async-start | bytes 1179648
  644.0 126.8 %reduce-scatter.26.cloned.1.call-start = ((), (), s32[]{:S(2)}) async-start(), calls=%async_computation.23 | async-start | bytes 417792
  645.3 201.9 %reduce-scatter.16.cloned.1.call-start = ((), (), s32[]{:S(2)}) async-start(), calls=%async_computation.18 | async-start | bytes 1671168 | tf_op jit(solution)/shard_map/reduce_scatter | solution.py:296
  663.8 259.9 %reduce-scatter.18.cloned.1.call-start = ((), (), s32[]{:S(2)}) async-start(), calls=%async_computation.19 | async-start | bytes 1671168 | tf_op jit(solution)/shard_map/reduce_scatter | solution.py:299
  697.3 308.2 %reduce-scatter.14.cloned.1.call-start = ((), (), s32[]{:S(2)}) async-start(), calls=%async_computation.17 | async-start | bytes 5013504 | tf_op jit(solution)/shard_map/reduce_scatter | solution.py:293
  726.5 361.1 %reduce-scatter.20.cloned.1.call-start = ((), (), s32[]{:S(2)}) async-start(), calls=%async_computation.20 | async-start | bytes 5013504 | tf_op jit(solution)/shard_map/reduce_scatter | solution.py:302
  731.1 513.2 %all-reduce.15.cloned.1.call-start = ((), (), s32[]{:S(2)}) async-start(), calls=%async_computation.24 | async-start | bytes 18874368 | tf_op jit(solution)/shard_map/psum | solution.py:209
  750.3 555.5 %all-reduce.17.cloned.1.call-start = ((), (), s32[]{:S(2)}) async-start(), calls=%async_computation.25 | async-start | bytes 1572864 | tf_op jit(solution)/shard_map/psum | solution.py:314
  756.0 331.6 %copy-start.47 = (f32[128]{0:T(128)S(1)}, f32[128]{0:T(128)}, u32[]{:S(2)}) copy-start(f32[128]{0:T(128)} %get-tuple-element.158) | copy-start | bytes 1540
  (48 other events, 715.9 us)
Sparse Core Ops, SparseCore 0:
  10.2 46.3 all-gather.9
  58.7 43.3 all-gather.13
  104.4 23.9 all-gather.11
  130.4 53.6 all-gather.17
  186.1 23.2 all-gather.15
  211.5 54.7 all-gather.19
  635.0 25.7 reduce-scatter.21
  663.8 30.6 reduce-scatter.23
  698.2 72.5 reduce-scatter.25
  774.2 72.9 reduce-scatter.15
  850.7 72.9 reduce-scatter.17
  927.9 77.5 reduce-scatter.13
  1009.8 77.7 reduce-scatter.19
  1092.8 151.3 all-reduce.14
  1246.7 59.1 all-reduce.16
where the time goes:
time: 1330 us; the launch traced here: 1320 us
  waiting for transfers between devices  730 us (55%)
  local copies, waits for them, and re-layouts  167 us (13%)
  matrix products  161 us (12%)
  blocking collectives  132 us (10%)
  other arithmetic  87.2 us (7%)
  starting transfers between devices  25.3 us (2%)
  between operations  17 us (1%)
    psum x1, waiting for transfers between devices, per_device(): lax.psum(grad_w_gate.astype(jnp.bfloat16), 'dp').astype(jnp.float32)  156 us
    reduce_scatter x1, waiting for transfers between devices, per_device(): lax.psum_scatter(grad_w_out.astype(jnp.bfloat16), 'dp', scatter_dimension...  82.1 us
    reduce_scatter x1, waiting for transfers between devices, per_device(): lax.psum_scatter(grad_w_query.astype(jnp.bfloat16), 'dp', scatter_dimensi...  81.7 us
    unnamed x3, blocking collectives  78.7 us
    reduce_scatter x1, waiting for transfers between devices, per_device(): lax.psum_scatter(grad_w_value.astype(jnp.bfloat16), 'dp', scatter_dimensi...  76.5 us
    unnamed x18, waiting for transfers between devices  63.3 us
    psum x1, waiting for transfers between devices, per_device(): lax.psum(shares[1].astype(jnp.bfloat16), 'expert').astype(jnp.float32)  48.8 us
    all_gather x1, waiting for transfers between devices, per_device(): lax.all_gather(w_out, 'dp', axis=0, tiled=True)  44.5 us
  transfers between devices with their start and end apart: 19, of which 17 were waited for; matrix products, arithmetic and copies ran while one was open for 22% of the time, Pallas kernels for 0%

commit v1 on v0

v1 whole, which is shorter than its diff:
```python
import jax
import jax.numpy as jnp
from jax import lax
from jax.sharding import Mesh, PartitionSpec as P

HEADS = 24
KV_HEADS = 8
HEAD_DIM = 64
GROUP = HEADS // KV_HEADS
TOP = 8
EXPERTS = 16

eps = 1e-06
residual_scale = 0.22
score_scale = 0.015625
rope_base = 10000.0
doc_slots = 3

bf16 = jnp.bfloat16
f32 = jnp.float32


def shift(value, axis, amount):
    size = lax.axis_size(axis)
    return lax.ppermute(value, axis, [((i + amount) % size, i) for i in range(size)])


def swap(value):
    return lax.ppermute(value, "core", [(0, 1), (1, 0)])


def dot(a, b, dims, out=f32):
    return lax.dot_general(a, b, (dims, ((), ())), preferred_element_type=out)


def turned(stacked, start):
    return lax.dynamic_slice_in_dim(
        jnp.concatenate([stacked, stacked], axis=0), start, stacked.shape[0], axis=0
    )


def gather_expert(block):
    far = [block] + [shift(block, "x", m) for m in (1, 2, 3)]
    mine = jnp.stack(far)
    return jnp.stack([mine, swap(mine)], axis=1)


def scatter_expert(parts):
    near = parts[:, 0].astype(f32) + swap(parts[:, 1]).astype(f32)
    low = near.astype(bf16)
    total = near[0]
    for m in (1, 2, 3):
        total = total + shift(low[m], "x", -m).astype(f32)
    return total


def gather_dp(block):
    row = jnp.stack([block] + [shift(block, "y", m) for m in (1, 2, 3)])
    y, z = lax.axis_index("y"), lax.axis_index("z")
    row = turned(row, (4 - y) % 4)
    whole = jnp.stack([row] + [shift(row, "z", m) for m in (1, 2, 3)])
    whole = turned(whole, (4 - z) % 4)
    return whole.reshape((16,) + block.shape)


def inverse_rms(values):
    return lax.rsqrt(jnp.mean(values * values, axis=-1, keepdims=True) + eps)


def rotate(values, cosine, sine):
    half_dim = values.shape[-1] // 2
    first_half = values[..., :half_dim]
    second_half = values[..., half_dim:]
    return jnp.concatenate(
        [
            first_half * cosine - second_half * sine,
            second_half * cosine + first_half * sine,
        ],
        axis=-1,
    )


def per_device(
    tokens,
    segments,
    routes,
    gain_attn,
    w_query,
    w_key,
    w_value,
    w_out,
    gain_moe,
    w_router,
    expert_gate,
    expert_up,
    expert_down,
    out_grad,
):
    rows, width = tokens.shape
    parts = 8
    seq = rows * parts
    x, core = lax.axis_index("x"), lax.axis_index("core")
    me = x * 2 + core
    q_cols = GROUP * HEAD_DIM

    share = jnp.concatenate(
        [
            lax.dynamic_slice_in_dim(w_query, me * q_cols, q_cols, axis=1),
            lax.dynamic_slice_in_dim(w_key, me * HEAD_DIM, HEAD_DIM, axis=1),
            lax.dynamic_slice_in_dim(w_value, me * HEAD_DIM, HEAD_DIM, axis=1),
            gain_attn[:, None],
            gain_moe[:, None],
            w_router,
            jnp.zeros((gain_attn.shape[0], 46), bf16),
        ],
        axis=1,
    )
    out_w = lax.all_gather(w_out, ("z", "y"), axis=0, tiled=True)
    sent = jnp.concatenate(
        [tokens, jnp.broadcast_to(segments.astype(bf16)[:, None], (rows, 128))], axis=1
    )
    everyone = gather_expert(sent).reshape(seq, width + 128)
    whole = gather_dp(share).reshape(width, 384)
    qkv_w = whole[:, : q_cols + 2 * HEAD_DIM]
    gain_one = whole[:, 320].astype(f32)
    gain_two = whole[:, 321].astype(f32)
    router_w = whole[:, 322:338]

    grad_sent, everyone = lax.optimization_barrier((out_grad, everyone))
    grad_all = gather_expert(grad_sent).reshape(seq, width)

    inputs_all = everyone[:, :width].astype(f32)
    seg_all = everyone[:, width].astype(jnp.int32)
    chips = (x + jnp.arange(4, dtype=jnp.int32)) % 4
    cores = jnp.bitwise_xor(core, jnp.arange(2, dtype=jnp.int32))
    place = (
        (chips[:, None, None] * 2 + cores[None, :, None]) * rows
        + jnp.arange(rows, dtype=jnp.int32)[None, None, :]
    ).reshape(seq)
    first = jnp.sum((seg_all < 1).astype(jnp.int32))
    second_start = jnp.sum((seg_all < 2).astype(jnp.int32))
    positions = place - jnp.where(
        seg_all == 0, 0, jnp.where(seg_all == 1, first, second_start)
    )
    half_dim = HEAD_DIM // 2
    inv_freq = rope_base ** (-jnp.arange(half_dim, dtype=f32) * 2.0 / HEAD_DIM)
    angles = positions.astype(f32)[:, None] * inv_freq[None, :]
    cosine, sine = jnp.cos(angles), jnp.sin(angles)

    scale_all = inverse_rms(inputs_all)
    normed = (inputs_all * scale_all * gain_one[None, :]).astype(bf16)
    qkv = dot(normed, qkv_w, ((1,), (0,)))
    queries = rotate(
        qkv[:, :q_cols].reshape(seq, GROUP, HEAD_DIM), cosine[:, None], sine[:, None]
    ).astype(bf16)
    keys = rotate(qkv[:, q_cols : q_cols + HEAD_DIM], cosine, sine).astype(bf16)
    values = qkv[:, q_cols + HEAD_DIM :].astype(bf16)
    allowed = (seg_all[:, None] == seg_all[None, :]) & (place[:, None] >= place[None, :])
    raw = jnp.einsum("qrd,kd->rqk", queries, keys, preferred_element_type=f32)
    scores = jnp.where(allowed[None], raw * score_scale, -1e30)
    maximum = jnp.max(scores, axis=-1, keepdims=True)
    exponent = jnp.exp(scores - maximum)
    denom = jnp.sum(exponent, axis=-1, keepdims=True)
    log_total = maximum + jnp.log(denom)
    probs = (exponent / denom).astype(bf16)
    mixed_head = jnp.einsum("rqk,kd->qrd", probs, values, preferred_element_type=f32).astype(bf16)

    by_owner = turned(mixed_head.reshape(4, 2, rows, q_cols), (4 - x) % 4)
    by_owner = jnp.where(core == 0, by_owner, by_owner[:, ::-1]).reshape(parts, rows, q_cols)
    mixed = lax.all_to_all(by_owner, ("x", "core"), 0, 0, tiled=True)
    mixed = mixed.transpose(1, 0, 2).reshape(rows, HEADS * HEAD_DIM)

    inputs = tokens.astype(f32)
    hidden = inputs + residual_scale * dot(mixed, out_w, ((1,), (0,)))
    scale_two = inverse_rms(hidden)
    second = (hidden * scale_two * gain_two[None, :]).astype(bf16)
    logits = dot(second, router_w, ((1,), (0,)))
    named = jnp.any(
        routes[:, :, None] == jnp.arange(EXPERTS, dtype=jnp.int32)[None, None, :], axis=1
    )
    gates = jax.nn.softmax(jnp.where(named, logits, -1e30), axis=1)
    gates = jnp.where(named, gates, 0.0)
    gates_high = gates.astype(bf16)
    gates_low = (gates - gates_high.astype(f32)).astype(bf16)
    sent_two = jnp.concatenate(
        [second, gates_high, gates_low, jnp.zeros((rows, 96), bf16)], axis=1
    )
    second_all = gather_expert(sent_two).reshape(seq, width + 128)

    gate_table = second_all[:, width : width + 16].astype(f32) + second_all[
        :, width + 16 : width + 32
    ].astype(f32)
    second_rows = second_all[:, :width]
    mine = (
        jnp.arange(EXPERTS, dtype=jnp.int32)[None, :]
        == 2 * me + jnp.arange(2, dtype=jnp.int32)[:, None]
    ).astype(f32)
    weight = jnp.sum(gate_table[None] * mine[:, None, :], axis=2)
    back = jnp.einsum("td,efd->etf", grad_all, expert_down, preferred_element_type=f32)
    gate_pre = jnp.einsum("td,edf->etf", second_rows, expert_gate, preferred_element_type=f32)
    up_pre = jnp.einsum("td,edf->etf", second_rows, expert_up, preferred_element_type=f32)
    sigmoid_gate = jax.nn.sigmoid(gate_pre)
    silu_gate = gate_pre * sigmoid_gate
    act = silu_gate * up_pre
    weighted = (act * weight[:, :, None]).astype(bf16)
    grad_gates = residual_scale * jnp.sum(act * back, axis=2)
    grad_act = back * (residual_scale * weight)[:, :, None]
    grad_gate_pre = (
        grad_act * up_pre * sigmoid_gate * (1.0 + gate_pre * (1.0 - sigmoid_gate))
    ).astype(bf16)
    grad_up_pre = (grad_act * silu_gate).astype(bf16)
    grad_w_down = residual_scale * jnp.einsum(
        "etf,td->efd", weighted, grad_all, preferred_element_type=f32
    )
    grad_w_gate = jnp.einsum("td,etf->edf", second_rows, grad_gate_pre, preferred_element_type=f32)
    grad_w_up = jnp.einsum("td,etf->edf", second_rows, grad_up_pre, preferred_element_type=f32)
    sums = lax.psum(
        (grad_w_gate.astype(bf16), grad_w_up.astype(bf16), grad_w_down.astype(bf16)), ("z", "y")
    )
    grad_rows = (
        jnp.einsum("etf,edf->td", grad_gate_pre, expert_gate, preferred_element_type=f32)
        + jnp.einsum("etf,edf->td", grad_up_pre, expert_up, preferred_element_type=f32)
    ).astype(bf16)
    routed = jnp.sum(grad_gates[:, :, None] * mine[:, None, :], axis=0)
    routed_high = routed.astype(bf16)
    routed_low = (routed - routed_high.astype(f32)).astype(bf16)
    grad_parts = jnp.concatenate(
        [grad_rows, routed_high, routed_low, jnp.zeros((seq, 96), bf16)], axis=1
    )
    grad_mine = scatter_expert(grad_parts.reshape(4, 2, rows, width + 128))
    combined = jnp.einsum("etf,efd->td", weighted, expert_down, preferred_element_type=f32)
    combined = combined.astype(bf16)
    combined, grad_mine = lax.optimization_barrier((combined, grad_mine))
    output = (
        hidden + residual_scale * scatter_expert(combined.reshape(4, 2, rows, width))
    ).astype(bf16)

    grad_second = grad_mine[:, :width]
    grad_gate_table = (
        grad_mine[:, width : width + 16] + grad_mine[:, width + 16 : width + 32]
    )
    grad_logits = gates * (
        grad_gate_table - jnp.sum(gates * grad_gate_table, axis=1, keepdims=True)
    )
    grad_logits_low = grad_logits.astype(bf16)
    grad_router = dot(second, grad_logits_low, ((0,), (0,)))
    grad_second = grad_second + dot(grad_logits_low, router_w, ((1,), (1,)))
    scaled_two = grad_second * gain_two[None, :]
    grad_gain_two = jnp.sum(grad_second * hidden * scale_two, axis=0)
    grad_final = out_grad.astype(f32)
    grad_hidden = (
        grad_final
        + scale_two * scaled_two
        - hidden * scale_two**3 * jnp.mean(hidden * scaled_two, axis=-1, keepdims=True)
    )
    grad_branch = (residual_scale * grad_hidden).astype(bf16)
    grad_mixed = dot(grad_branch, out_w, ((1,), (1,))).astype(bf16)

    def to_heads(value):
        blocks = value.reshape(rows, parts, q_cols).transpose(1, 0, 2)
        return lax.all_to_all(blocks, ("x", "core"), 0, 0, tiled=True)

    def from_here(blocks):
        blocks = turned(blocks.reshape(4, 2, rows, q_cols), x)
        return jnp.where(core == 0, blocks, blocks[:, ::-1]).reshape(seq, q_cols)

    grad_four = from_here(to_heads(grad_mixed)).reshape(seq, GROUP, HEAD_DIM)

    again = jnp.exp(scores - log_total)
    grad_probs = jnp.einsum("qrd,kd->rqk", grad_four, values, preferred_element_type=f32)
    delta = jnp.sum(again * grad_probs, axis=-1, keepdims=True)
    grad_raw = (again * (grad_probs - delta) * score_scale).astype(bf16)
    grad_q = jnp.einsum("rqk,kd->qrd", grad_raw, keys, preferred_element_type=f32)
    grad_k = jnp.einsum("rqk,qrd->kd", grad_raw, queries, preferred_element_type=f32)
    grad_v = jnp.einsum("rqk,qrd->kd", again.astype(bf16), grad_four, preferred_element_type=f32)
    grad_qkv = jnp.concatenate(
        [
            rotate(grad_q, cosine[:, None], -sine[:, None]).astype(bf16).reshape(seq, q_cols),
            rotate(grad_k, cosine, -sine).astype(bf16),
            grad_v.astype(bf16),
        ],
        axis=1,
    )
    grad_normed = dot(grad_qkv, qkv_w, ((1,), (1,)))
    grad_gain_one = jnp.sum(grad_normed * inputs_all * scale_all, axis=0)
    grad_w_qkv = dot(normed, grad_qkv, ((0,), (0,)))
    normed_mine = scatter_expert(grad_normed.astype(bf16).reshape(4, 2, rows, width))
    scale_one = inverse_rms(inputs)
    scaled_one = normed_mine * gain_one[None, :]
    grad_inputs = (
        grad_hidden
        + scale_one * scaled_one
        - inputs * scale_one**3 * jnp.mean(inputs * scaled_one, axis=-1, keepdims=True)
    )

    mixed_sent, second_all = lax.optimization_barrier((mixed, second_all))
    mixed_all = lax.all_gather(mixed_sent, ("x", "core"), axis=0, tiled=True)
    branch_cols = to_heads(grad_branch).reshape(seq, q_cols)
    grad_w_out = dot(mixed_all, branch_cols, ((0,), (0,)))

    table = jnp.concatenate(
        [
            grad_w_qkv.astype(bf16),
            grad_w_out.astype(bf16),
            grad_gain_one.astype(bf16)[:, None],
            grad_gain_two.astype(bf16)[:, None],
            grad_router.astype(bf16),
            jnp.zeros((width, 110), bf16),
        ],
        axis=1,
    ).reshape(16, width // 16, 640)
    pieces = lax.all_to_all(table, ("z", "y"), 0, 0, tiled=True)
    summed = jnp.sum(pieces.astype(f32), axis=0).astype(bf16)
    lines = gather_expert(summed)
    lines = turned(lines, (4 - x) % 4)
    lines = jnp.where(core == 0, lines, lines[:, ::-1]).reshape(parts, width // 16, 640)
    lines = lines.astype(f32)
    side = lambda a, b: lines[:, :, a:b].transpose(1, 0, 2).reshape(width // 16, parts * (b - a))
    rest = jnp.sum(lines[:, :, 512:530], axis=0)
    return (
        output,
        grad_inputs,
        rest[:, 0],
        side(0, 192),
        side(192, 256),
        side(256, 320),
        side(320, 512),
        rest[:, 1],
        rest[:, 2:18],
        sums[0].astype(f32),
        sums[1].astype(f32),
        sums[2].astype(f32),
    )


def solution(mesh):
    fine = Mesh(mesh.devices.reshape(4, 4, 4, 2), ("z", "y", "x", "core"))
    dp, expert, both = ("z", "y"), ("x", "core"), ("z", "y", "x", "core")
    return jax.shard_map(
        per_device,
        mesh=fine,
        in_specs=(
            P(both, None),
            P(both),
            P(both, None),
            P(dp),
            P(dp, None),
            P(dp, None),
            P(dp, None),
            P(dp, None),
            P(dp),
            P(dp, None),
            P(expert, None, None),
            P(expert, None, None),
            P(expert, None, None),
            P(both, None),
        ),
        out_specs=(
            P(both, None),
            P(both, None),
            P(dp),
            P(dp, None),
            P(dp, None),
            P(dp, None),
            P(dp, None),
            P(dp),
            P(dp, None),
            P(expert, None, None),
            P(expert, None, None),
            P(expert, None, None),
        ),
        check_vma=False,
    )
```

time: 1330 us -> 535 us (0.40)
  waiting for transfers between devices: 730 us -> 104 us
  blocking collectives: 132 us -> 0 us
  starting transfers between devices: 25.3 us -> 79.8 us
  local copies, waits for them, and re-layouts: 167 us -> 115 us
  matrix products: 161 us -> 141 us
  other arithmetic: 87.2 us -> 70 us
    reduce_scatter x4 -> x0, waiting for transfers between devices: 257 us -> none  [the longest x1 82.1 us: per_device(): lax.psum_scatter(grad_w_out.astype(jnp.bfloat16), 'dp', scatter_dimension...]
    psum x2 -> x1, waiting for transfers between devices: 204 us -> 0.01 us  [per_device(): lax.psum((grad_w_gate.astype(bf16), grad_w_up.astype(bf16), grad_w_down.a...]
    all_gather x6 -> x2, waiting for transfers between devices: 105 us -> 0.01 us  [the longest x1 0.01 us: per_device(): out_w = lax.all_gather(w_out, ('z', 'y'), axis=0, tiled=True)]
    ppermute x0 -> x34, waiting for transfers between devices: none -> 89 us  [the longest x27 88.7 us: shift(): lax.ppermute(value, axis, [((i + amount) % size, i) for i in range(size)])]
    all_to_all x4, waiting for transfers between devices: 100 us -> 14.9 us  [the longest x1 10.3 us: per_device(): pieces = lax.all_to_all(table, ('z', 'y'), 0, 0, tiled=True)]
    gather x9 -> x0, local copies, waits for them, and re-layouts: 80.4 us -> none  [the longest x1 22.9 us: per_device(): grad_back[flat_routes, slot_of].reshape(rows_here, TOP, width)]
    unnamed x3 -> x0, blocking collectives: 78.7 us -> none
    unnamed x18 -> x3, waiting for transfers between devices: 63.3 us -> 0.05 us
  transfers between devices with their start and end apart: 19 -> 41, of which waited for: 17 -> 20; matrix products, arithmetic and copies ran while one was open for 22% -> 45% of each run, Pallas kernels for 0% -> 0%
where the time goes in v1:
time: 535 us; the launch traced here: 525 us
  matrix products  141 us (26%)
  local copies, waits for them, and re-layouts  115 us (21%)
  waiting for transfers between devices  104 us (19%)
  starting transfers between devices  79.8 us (15%)
  other arithmetic  70 us (13%)
  between operations  15.5 us (3%)
    ppermute x27, waiting for transfers between devices, shift(): lax.ppermute(value, axis, [((i + amount) % size, i) for i in range(size)])  88.7 us
    unnamed x176, local copies, waits for them, and re-layouts  48 us
    ppermute x27, starting transfers between devices, shift(): lax.ppermute(value, axis, [((i + amount) % size, i) for i in range(size)])  32.2 us
    dot_general x9, matrix products, dot(): return lax.dot_general(a, b, (dims, ((), ())), preferred_element_type=out)  25.9 us
    ppermute x7, starting transfers between devices, swap(): return lax.ppermute(value, 'core', [(0, 1), (1, 0)])  25.8 us
    dot_general x1, matrix products, per_device(): jnp.einsum('rqk,kd->qrd', grad_raw, keys, preferred_element_type=f32)  20 us
    dot_general x1, matrix products, per_device(): jnp.einsum('rqk,qrd->kd', grad_raw, queries, preferred_element_type=f32)  19.9 us
    another operation x6, other arithmetic, gather_expert(): return jnp.stack([mine, swap(mine)], axis=1)  13.2 us
  transfers between devices with their start and end apart: 41, of which 20 were waited for; matrix products, arithmetic and copies ran while one was open for 45% of the time, Pallas kernels for 0%

profile of v1, /device:TPU:1, one launch (start us, length us, event | category | flops | bytes accessed | tf_op | source)
XLA Modules:
  0.0 524.5 jit_solution(6985309290181515034)
XLA Ops:
  37.9 6.8 %collective-permute-done.7 = bf16[4,96,384]{2,1,0:T(8,128)(2,1)} collective-permute-done((bf16[4,96,384]{2,1,0:T(8,128)(2,1)}, bf16[4,96,384]{2,1,0:T(8,128)(2,1)}, u32[]{:S(2)}, u32[]{:S(2)}) %collective-permute-start.7) | collective-permute-done | bytes 294944 | tf_op jit(solution)/shard_map/ppermute | solution.py:25
  48.4 8.3 %collective-permute-start.3 = (bf16[4,128,1664]{2,1,0:T(8,128)(2,1)S(1)}, bf16[4,128,1664]{2,1,0:T(8,128)(2,1)S(1)}, u32[]{:S(2)}, u32[]{:S(2)}) collective-permute-start(bf16[4,128,1664]{2,1,0:T(8,128)(2,1)S(1)} %get-tuple-element.166), channel_id=1, source_target_pairs={{0,1},{1,0},{2,3},{3,2},{4,5},{5,4},{6,7},{7,6},{8,9},{9,8},{10,11... | collective-permute-start | bytes 5111816 | tf_op jit(solution)/shard_map/ppermute | solution.py:29
  95.2 9.0 %all-to-all-start = ((bf16[8,128,192]{1,2,0:T(8,128)(2,1)}), bf16[8,128,192]{1,2,0:T(8,128)(2,1)}, u32[]{:S(2)}, u32[]{:S(2)}) async-start(bf16[8,128,192]{1,2,0:T(8,128)(2,1)} %bitcast.347), calls=%async_computation | async-start | bytes 786432 | tf_op jit(solution)/shard_map/all_to_all | solution.py:170
  122.9 9.2 %collective-permute-done.12 = bf16[128,1664]{0,1:T(8,128)(2,1)S(1)} collective-permute-done((bf16[128,1664]{0,1:T(8,128)(2,1)S(1)}, bf16[128,1664]{0,1:T(8,128)(2,1)S(1)}, u32[]{:S(2)}, u32[]{:S(2)}) %collective-permute-start.12) | collective-permute-done | bytes 426016 | tf_op jit(solution)/shard_map/ppermute | solution.py:25
  132.1 7.9 %collective-permute-done.11 = bf16[128,1664]{0,1:T(8,128)(2,1)S(1)} collective-permute-done((bf16[128,1664]{0,1:T(8,128)(2,1)S(1)}, bf16[128,1664]{0,1:T(8,128)(2,1)S(1)}, u32[]{:S(2)}, u32[]{:S(2)}) %collective-permute-start.11) | collective-permute-done | bytes 426016 | tf_op jit(solution)/shard_map/ppermute | solution.py:25
  143.1 10.3 %collective-permute-start.13 = (bf16[4,128,1664]{1,2,0:T(8,128)(2,1)}, bf16[4,128,1664]{1,2,0:T(8,128)(2,1)}, u32[]{:S(2)}, u32[]{:S(2)}) collective-permute-start(bf16[4,128,1664]{1,2,0:T(8,128)(2,1)} %get-tuple-element.164), channel_id=1, source_target_pairs={{0,1},{1,0},{2,3},{3,2},{4,5},{5,4},{6,7},{7,6},{8,9},{9,8},{10,11... | collective-permute-start | bytes 5111816 | tf_op jit(solution)/shard_map/ppermute | solution.py:29
  168.8 6.5 %fusion.48 = f32[1024,2,512]{0,2,1:T(8,128)S(1)} fusion(bf16[2,1536,512]{2,1,0:T(8,128)(2,1)} %param.25, bf16[1024,1664]{1,0:T(8,128)(2,1)} %bitcast.333), kind=kOutput, calls=%fused_computation.92 | convolution fusion | flops 3221225472 | bytes 10485760 | tf_op jit(solution)/shard_map/td,edf->etf/dot_general | solution.py:201
  185.7 7.7 %multiply_convert_fusion.1 = (bf16[2,1024,512]{1,2,0:T(8,128)(2,1)}, bf16[2,1024,512]{1,2,0:T(8,128)(2,1)S(1)}, bf16[2,1024,512]{1,2,0:T(8,128)(2,1)}) fusion(f32[1024,2,512]{0,2,1:T(8,128)} %get-tuple-element.207, f32[2,1024]{1,0:T(2,128)S(1)} %broadcast_multiply_fusion.1, f32[1024,2,512]{0,2,1:T(8,128)} %copy-done.17, f32[1024,2,512]{0,2,1:T(8,128)} %copy-done.16, ...), kind=kLoop, calls=%fused_computation.42 | loop fusion | flops 17825792 | bytes 18890752 | tf_op jit(solution)/shard_map/convert_element_type | solution.py:211
  193.5 5.6 %fusion.122 = f32[1024,1536,1]{1,0,2:T(8,128)} fusion(bf16[2,1024,512]{1,2,0:T(8,128)(2,1)S(1)} %get-tuple-element.138, bf16[2,1536,512]{2,1,0:T(8,128)(2,1)S(1)} %copy-done.69), kind=kOutput, calls=%fused_computation.266 | convolution fusion | flops 3221225472 | bytes 11534336 | tf_op jit(solution)/shard_map/etf,edf->td/dot_general | solution.py:221
  200.1 9.5 %fusion.13 = bf16[1024,1536]{1,0:T(8,128)(2,1)} fusion(f32[1024,1536,1]{1,0,2:T(8,128)} %fusion.122, bf16[2,1024,512]{1,2,0:T(8,128)(2,1)} %get-tuple-element.137, bf16[2,1536,512]{2,1,0:T(8,128)(2,1)} %param.25), kind=kOutput, calls=%fused_computation.22 | convolution fusion | flops 3224371200 | bytes 14680064 | tf_op jit(solution)/shard_map/etf,edf->td/dot_general | solution.py:222
  210.4 6.5 %concatenate.65 = bf16[1024,1664]{1,0:T(8,128)(2,1)} concatenate(bf16[1024,1536]{1,0:T(8,128)(2,1)} %fusion.13, bf16[1024,16]{1,0:T(8,128)(2,1)S(1)} %copy.331, bf16[1024,16]{1,0:T(8,128)(2,1)} %copy.332, bf16[1024,96]{1,0:T(8,128)(2,1)} %broadcast_in_dim.54), dimensions={1} | concatenate | bytes 6815744 | tf_op jit(solution)/shard_map/concatenate | solution.py:227
  240.1 8.4 %collective-permute-done.21 = bf16[128,1664]{0,1:T(8,128)(2,1)S(1)} collective-permute-done((bf16[128,1664]{0,1:T(8,128)(2,1)S(1)}, bf16[128,1664]{0,1:T(8,128)(2,1)S(1)}, u32[]{:S(2)}, u32[]{:S(2)}) %collective-permute-start.21) | collective-permute-done | bytes 426016 | tf_op jit(solution)/shard_map/ppermute | solution.py:25
  251.6 14.2 %collective-permute-done.19 = bf16[128,1664]{0,1:T(8,128)(2,1)S(1)} collective-permute-done((bf16[128,1664]{0,1:T(8,128)(2,1)S(1)}, bf16[128,1664]{0,1:T(8,128)(2,1)S(1)}, u32[]{:S(2)}, u32[]{:S(2)}) %collective-permute-start.19) | collective-permute-done | bytes 426016 | tf_op jit(solution)/shard_map/ppermute | solution.py:25
  270.0 8.0 %fusion.27 = bf16[2,1536,512]{1,2,0:T(8,128)(2,1)} fusion(bf16[2,1024,512]{1,2,0:T(8,128)(2,1)} %copy-done.24, bf16[1024,1664]{1,0:T(8,128)(2,1)} %bitcast.334), kind=kOutput, calls=%fused_computation.53 | convolution fusion | flops 3222798336 | bytes 8388608 | tf_op jit(solution)/shard_map/td,etf->edf/dot_general | solution.py:215
  290.7 6.8 %collective-permute-done.25 = bf16[128,1536]{0,1:T(8,128)(2,1)S(1)} collective-permute-done((bf16[128,1536]{0,1:T(8,128)(2,1)S(1)}, bf16[128,1536]{0,1:T(8,128)(2,1)S(1)}, u32[]{:S(2)}, u32[]{:S(2)}) %collective-permute-start.25) | collective-permute-done | bytes 393248 | tf_op jit(solution)/shard_map/ppermute | solution.py:25
  298.7 9.2 %collective-permute-done.23 = bf16[128,1536]{0,1:T(8,128)(2,1)S(1)} collective-permute-done((bf16[128,1536]{0,1:T(8,128)(2,1)S(1)}, bf16[128,1536]{0,1:T(8,128)(2,1)S(1)}, u32[]{:S(2)}, u32[]{:S(2)}) %collective-permute-start.23) | collective-permute-done | bytes 393248 | tf_op jit(solution)/shard_map/ppermute | solution.py:25
  316.8 7.6 %multiply_convert_fusion = bf16[2,512,1536]{2,1,0:T(8,128)(2,1)} fusion(bf16[2,1024,512]{1,2,0:T(8,128)(2,1)} %get-tuple-element.139, bf16[1024,1536,1]{1,0,2:T(8,128)(2,1)} %bitcast.337), kind=kOutput, calls=%fused_computation.24 | convolution fusion | flops 3224371200 | bytes 8388608 | tf_op jit(solution)/shard_map/etf,td->efd/dot_general | solution.py:212
  330.7 7.4 %fusion.92 = f32[1024,1024,3]{1,0,2:T(8,128)} fusion(bf16[1024,3,64]{0,2,1:T(8,128)(2,1)S(1)} %reshape_reshape.7, f32[1024,320]{0,1:T(8,128)} %copy-done.25), kind=kOutput, calls=%fused_computation.206 | convolution fusion | flops 402653184 | bytes 13107200 | tf_op jit(solution)/shard_map/qrd,kd->rqk/dot_general | solution.py:270
  338.1 20.0 %fusion.30 = f32[1024,3,64]{0,2,1:T(8,128)S(1)} fusion(f32[1024,1024,3]{1,0,2:T(8,128)} %fusion.92, f32[3,1024,1024]{1,2,0:T(8,128)} %copy-done.2, f32[3,1024]{1,0:T(4,128)S(1)} %copy-done.35, bf16[1024,32]{0,1:T(8,128)(2,1)S(1)} %copy-done.45, bf16[1024,32]{0,1:T(8,128)(2,1)S(1)} %copy-done.47), kind=kOutput, calls=%fused_computation.77 | convolution fusion | flops 424939520 | bytes 26095616 | tf_op jit(solution)/shard_map/rqk,kd->qrd/dot_general | solution.py:273
  358.3 19.9 %fusion.36 = f32[1024,64]{0,1:T(8,128)S(1)} fusion(f32[1024,1024,3]{1,0,2:T(8,128)} %fusion.92, f32[3,1024,1024]{1,2,0:T(8,128)} %copy-done.2, f32[3,1024]{1,0:T(4,128)S(1)} %copy-done.35, bf16[1024,3,32]{0,2,1:T(8,128)(2,1)} %copy-done.34, bf16[1024,3,32]{0,2,1:T(8,128)(2,1)} %copy-done.33), kind=kOutput, calls=%fused_computation.81 | convolution fusion | flops 425463808 | bytes 25833472 | tf_op jit(solution)/shard_map/rqk,qrd->kd/dot_general | solution.py:274
  378.9 7.1 %fusion.37 = bf16[1024,64]{0,1:T(8,128)(2,1)S(1)} fusion(bf16[1024,3,64]{0,2,1:T(8,128)(2,1)S(1)} %reshape_reshape.7, f32[3,1024,1024]{1,2,0:T(8,128)} %copy-done.2, f32[3,1024]{1,0:T(4,128)S(1)} %copy-done.35), kind=kOutput, calls=%fused_computation.82 | convolution fusion | flops 409010176 | bytes 13119488 | tf_op jit(solution)/shard_map/rqk,qrd->kd/dot_general | solution.py:275
  438.8 5.6 %collective-permute-done.29 = bf16[128,1536]{0,1:T(8,128)(2,1)} collective-permute-done((bf16[128,1536]{0,1:T(8,128)(2,1)}, bf16[128,1536]{0,1:T(8,128)(2,1)}, u32[]{:S(2)}, u32[]{:S(2)}) %collective-permute-start.29) | collective-permute-done | bytes 393248 | tf_op jit(solution)/shard_map/ppermute | solution.py:25
  447.3 9.7 %collective-permute-done.27 = bf16[128,1536]{0,1:T(8,128)(2,1)} collective-permute-done((bf16[128,1536]{0,1:T(8,128)(2,1)}, bf16[128,1536]{0,1:T(8,128)(2,1)}, u32[]{:S(2)}, u32[]{:S(2)}) %collective-permute-start.27) | collective-permute-done | bytes 393248 | tf_op jit(solution)/shard_map/ppermute | solution.py:25
  460.0 10.3 %all-to-all-done.3 = bf16[16,96,640]{2,1,0:T(8,128)(2,1)S(1)} async-done(((bf16[16,96,640]{2,1,0:T(8,128)(2,1)}), bf16[16,96,640]{2,1,0:T(8,128)(2,1)S(1)}, u32[]{:S(2)}, u32[]{:S(2)}) %all-to-all-start.3) | async-done | bytes 1966112 | tf_op jit(solution)/shard_map/all_to_all | solution.py:312
  (378 shorter events, 287.3 us)
Async XLA Ops:
  7.2 105.3 %all-gather.3.cloned.1.call-start = ((), (), s32[]{:S(2)}) async-start(), calls=%async_computation.4 | async-start | bytes 5013504 | tf_op jit(solution)/shard_map/all_gather | solution.py:118
  19.1 27.4 %collective-permute-start.2 = (bf16[128,1664]{1,0:T(8,128)(2,1)}, bf16[128,1664]{1,0:T(8,128)(2,1)}, u32[]{:S(2)}, u32[]{:S(2)}) collective-permute-start(bf16[128,1664]{1,0:T(8,128)(2,1)} %get-tuple-element.186), channel_id=1, source_target_pairs={{6,0},{0,2},{2,4},{4,6},{7,1},{1,3},{3,5},{5,7},{14,8},{8,10},{10,... | collective-permute-start | bytes 1277960 | tf_op jit(solution)/shard_map/ppermute | solution.py:25
  20.3 26.2 %collective-permute-start.1 = (bf16[128,1664]{1,0:T(8,128)(2,1)}, bf16[128,1664]{1,0:T(8,128)(2,1)}, u32[]{:S(2)}, u32[]{:S(2)}) collective-permute-start(bf16[128,1664]{1,0:T(8,128)(2,1)} %get-tuple-element.186), channel_id=1, source_target_pairs={{4,0},{6,2},{0,4},{2,6},{5,1},{7,3},{1,5},{3,7},{12,8},{14,10},{8,... | collective-permute-start | bytes 1277960 | tf_op jit(solution)/shard_map/ppermute | solution.py:25
  23.4 23.1 %collective-permute-start = (bf16[128,1664]{1,0:T(8,128)(2,1)}, bf16[128,1664]{1,0:T(8,128)(2,1)}, u32[]{:S(2)}, u32[]{:S(2)}) collective-permute-start(bf16[128,1664]{1,0:T(8,128)(2,1)} %get-tuple-element.186), channel_id=1, source_target_pairs={{2,0},{4,2},{6,4},{0,6},{3,1},{5,3},{7,5},{1,7},{10,8},{12,10},{14... | collective-permute-start | bytes 1277960 | tf_op jit(solution)/shard_map/ppermute | solution.py:25
  31.0 13.7 %collective-permute-start.7 = (bf16[4,96,384]{2,1,0:T(8,128)(2,1)}, bf16[4,96,384]{2,1,0:T(8,128)(2,1)}, u32[]{:S(2)}, u32[]{:S(2)}) collective-permute-start(bf16[4,96,384]{2,1,0:T(8,128)(2,1)} %get-tuple-element.136), channel_id=1, source_target_pairs={{32,0},{64,32},{96,64},{0,96},{33,1},{65,33},{97,65},{1,97},{34,2}... | collective-permute-start | bytes 884744 | tf_op jit(solution)/shard_map/ppermute | solution.py:25
  37.8 18.9 %collective-permute-start.8 = (bf16[4,96,384]{2,1,0:T(8,128)(2,1)}, bf16[4,96,384]{2,1,0:T(8,128)(2,1)S(1)}, u32[]{:S(2)}, u32[]{:S(2)}) collective-permute-start(bf16[4,96,384]{2,1,0:T(8,128)(2,1)} %get-tuple-element.136), channel_id=1, source_target_pairs={{64,0},{96,32},{0,64},{32,96},{65,1},{97,33},{1,65},{33,97},{66,2}... | collective-permute-start | bytes 884744 | tf_op jit(solution)/shard_map/ppermute | solution.py:25
  60.6 44.3 %collective-permute-start.16 = (bf16[128,1536]{1,0:T(8,128)(2,1)}, bf16[128,1536]{1,0:T(8,128)(2,1)}, u32[]{:S(2)}, u32[]{:S(2)}) collective-permute-start(bf16[128,1536]{1,0:T(8,128)(2,1)} %param.27), channel_id=1, source_target_pairs={{6,0},{0,2},{2,4},{4,6},{7,1},{1,3},{3,5},{5,7},{14,8},{8,10},{10,... | collective-permute-start | bytes 1179656 | tf_op jit(solution)/shard_map/ppermute | solution.py:25
  61.2 43.7 %collective-permute-start.15 = (bf16[128,1536]{1,0:T(8,128)(2,1)}, bf16[128,1536]{1,0:T(8,128)(2,1)}, u32[]{:S(2)}, u32[]{:S(2)}) collective-permute-start(bf16[128,1536]{1,0:T(8,128)(2,1)} %param.27), channel_id=1, source_target_pairs={{4,0},{6,2},{0,4},{2,6},{5,1},{7,3},{1,5},{3,7},{12,8},{14,10},{8,... | collective-permute-start | bytes 1179656 | tf_op jit(solution)/shard_map/ppermute | solution.py:25
  62.2 42.7 %collective-permute-start.14 = (bf16[128,1536]{1,0:T(8,128)(2,1)}, bf16[128,1536]{1,0:T(8,128)(2,1)}, u32[]{:S(2)}, u32[]{:S(2)}) collective-permute-start(bf16[128,1536]{1,0:T(8,128)(2,1)} %param.27), channel_id=1, source_target_pairs={{2,0},{4,2},{6,4},{0,6},{3,1},{5,3},{7,5},{1,7},{10,8},{12,10},{14... | collective-permute-start | bytes 1179656 | tf_op jit(solution)/shard_map/ppermute | solution.py:25
  95.2 17.2 %all-to-all-start = ((bf16[8,128,192]{1,2,0:T(8,128)(2,1)}), bf16[8,128,192]{1,2,0:T(8,128)(2,1)}, u32[]{:S(2)}, u32[]{:S(2)}) async-start(bf16[8,128,192]{1,2,0:T(8,128)(2,1)} %bitcast.347), calls=%async_computation | async-start | bytes 786432 | tf_op jit(solution)/shard_map/all_to_all | solution.py:170
  104.2 307.8 %all-gather.5.cloned.1.call-start = ((), (), s32[]{:S(2)}) async-start(), calls=%async_computation.5 | async-start | bytes 3538944 | tf_op jit(solution)/shard_map/all_gather | solution.py:297
  108.1 45.4 %collective-permute-start.17 = (bf16[4,128,1536]{2,1,0:T(8,128)(2,1)}, bf16[4,128,1536]{2,1,0:T(8,128)(2,1)}, u32[]{:S(2)}, u32[]{:S(2)}) collective-permute-start(bf16[4,128,1536]{2,1,0:T(8,128)(2,1)} %get-tuple-element.174), channel_id=1, source_target_pairs={{0,1},{1,0},{2,3},{3,2},{4,5},{5,4},{6,7},{7,6},{8,9},{9,8},{10,11... | collective-permute-start | bytes 4718600 | tf_op jit(solution)/shard_map/ppermute | solution.py:29
  120.1 19.9 %collective-permute-start.11 = (bf16[128,1664]{0,1:T(8,128)(2,1)S(1)}, bf16[128,1664]{0,1:T(8,128)(2,1)S(1)}, u32[]{:S(2)}, u32[]{:S(2)}) collective-permute-start(bf16[128,1664]{0,1:T(8,128)(2,1)S(1)} %maximum_maximum_fusion), channel_id=1, source_target_pairs={{4,0},{6,2},{0,4},{2,6},{5,1},{7,3},{1,5},{3,7},{12,8},{14,10},{8,... | collective-permute-start | bytes 1277960 | tf_op jit(solution)/shard_map/ppermute | solution.py:25
  121.9 19.2 %collective-permute-start.10 = (bf16[128,1664]{0,1:T(8,128)(2,1)S(1)}, bf16[128,1664]{0,1:T(8,128)(2,1)S(1)}, u32[]{:S(2)}, u32[]{:S(2)}) collective-permute-start(bf16[128,1664]{0,1:T(8,128)(2,1)S(1)} %maximum_maximum_fusion), channel_id=1, source_target_pairs={{2,0},{4,2},{6,4},{0,6},{3,1},{5,3},{7,5},{1,7},{10,8},{12,10},{14... | collective-permute-start | bytes 1277960 | tf_op jit(solution)/shard_map/ppermute | solution.py:25
  143.1 14.4 %collective-permute-start.13 = (bf16[4,128,1664]{1,2,0:T(8,128)(2,1)}, bf16[4,128,1664]{1,2,0:T(8,128)(2,1)}, u32[]{:S(2)}, u32[]{:S(2)}) collective-permute-start(bf16[4,128,1664]{1,2,0:T(8,128)(2,1)} %get-tuple-element.164), channel_id=1, source_target_pairs={{0,1},{1,0},{2,3},{3,2},{4,5},{5,4},{6,7},{7,6},{8,9},{9,8},{10,11... | collective-permute-start | bytes 5111816 | tf_op jit(solution)/shard_map/ppermute | solution.py:29
  233.4 15.1 %collective-permute-start.21 = (bf16[128,1664]{0,1:T(8,128)(2,1)S(1)}, bf16[128,1664]{0,1:T(8,128)(2,1)S(1)}, u32[]{:S(2)}, u32[]{:S(2)}) collective-permute-start(bf16[128,1664]{0,1:T(8,128)(2,1)S(1)} %get-tuple-element.161), channel_id=1, source_target_pairs={{2,0},{4,2},{6,4},{0,6},{3,1},{5,3},{7,5},{1,7},{10,8},{12,10},{14... | collective-permute-start | bytes 1277960 | tf_op jit(solution)/shard_map/ppermute | solution.py:25
  235.6 16.0 %collective-permute-start.20 = (bf16[128,1664]{0,1:T(8,128)(2,1)S(1)}, bf16[128,1664]{0,1:T(8,128)(2,1)S(1)}, u32[]{:S(2)}, u32[]{:S(2)}) collective-permute-start(bf16[128,1664]{0,1:T(8,128)(2,1)S(1)} %get-tuple-element.162), channel_id=1, source_target_pairs={{4,0},{6,2},{0,4},{2,6},{5,1},{7,3},{1,5},{3,7},{12,8},{14,10},{8,... | collective-permute-start | bytes 1277960 | tf_op jit(solution)/shard_map/ppermute | solution.py:25
  235.6 30.2 %collective-permute-start.19 = (bf16[128,1664]{0,1:T(8,128)(2,1)S(1)}, bf16[128,1664]{0,1:T(8,128)(2,1)S(1)}, u32[]{:S(2)}, u32[]{:S(2)}) collective-permute-start(bf16[128,1664]{0,1:T(8,128)(2,1)S(1)} %get-tuple-element.160), channel_id=1, source_target_pairs={{6,0},{0,2},{2,4},{4,6},{7,1},{1,3},{3,5},{5,7},{14,8},{8,10},{10,... | collective-permute-start | bytes 1277960 | tf_op jit(solution)/shard_map/ppermute | solution.py:25
  268.8 15.7 %collective-permute-start.22 = (bf16[4,128,1536]{1,2,0:T(8,128)(2,1)}, bf16[4,128,1536]{1,2,0:T(8,128)(2,1)}, u32[]{:S(2)}, u32[]{:S(2)}) collective-permute-start(bf16[4,128,1536]{1,2,0:T(8,128)(2,1)} %bitcast.346), channel_id=1, source_target_pairs={{0,1},{1,0},{2,3},{3,2},{4,5},{5,4},{6,7},{7,6},{8,9},{9,8},{10,11... | collective-permute-start | bytes 4718600 | tf_op jit(solution)/shard_map/ppermute | solution.py:29
  287.0 20.9 %collective-permute-start.23 = (bf16[128,1536]{0,1:T(8,128)(2,1)S(1)}, bf16[128,1536]{0,1:T(8,128)(2,1)S(1)}, u32[]{:S(2)}, u32[]{:S(2)}) collective-permute-start(bf16[128,1536]{0,1:T(8,128)(2,1)S(1)} %get-tuple-element.170), channel_id=1, source_target_pairs={{6,0},{0,2},{2,4},{4,6},{7,1},{1,3},{3,5},{5,7},{14,8},{8,10},{10,... | collective-permute-start | bytes 1179656 | tf_op jit(solution)/shard_map/ppermute | solution.py:25
  316.8 186.1 %all-reduce.3.cloned.1.call-start = ((), (), s32[]{:S(2)}) async-start(), calls=%async_computation.6 | async-start | bytes 18874368 | tf_op jit(solution)/shard_map/psum | solution.py:217
  393.4 34.8 %collective-permute-start.26 = (bf16[4,128,1536]{1,2,0:T(8,128)(2,1)}, bf16[4,128,1536]{1,2,0:T(8,128)(2,1)}, u32[]{:S(2)}, u32[]{:S(2)}) collective-permute-start(bf16[4,128,1536]{1,2,0:T(8,128)(2,1)} %bitcast.345), channel_id=1, source_target_pairs={{0,1},{1,0},{2,3},{3,2},{4,5},{5,4},{6,7},{7,6},{8,9},{9,8},{10,11... | collective-permute-start | bytes 4718600 | tf_op jit(solution)/shard_map/ppermute | solution.py:29
  423.2 47.0 %all-to-all-start.3 = ((bf16[16,96,640]{2,1,0:T(8,128)(2,1)}), bf16[16,96,640]{2,1,0:T(8,128)(2,1)S(1)}, u32[]{:S(2)}, u32[]{:S(2)}) async-start(bf16[16,96,640]{2,1,0:T(8,128)(2,1)} %concatenate.72), calls=%async_computation.3 | async-start | bytes 3932160 | tf_op jit(solution)/shard_map/all_to_all | solution.py:312
  436.3 20.7 %collective-permute-start.27 = (bf16[128,1536]{0,1:T(8,128)(2,1)}, bf16[128,1536]{0,1:T(8,128)(2,1)}, u32[]{:S(2)}, u32[]{:S(2)}) collective-permute-start(bf16[128,1536]{0,1:T(8,128)(2,1)} %get-tuple-element.167), channel_id=1, source_target_pairs={{6,0},{0,2},{2,4},{4,6},{7,1},{1,3},{3,5},{5,7},{14,8},{8,10},{10,... | collective-permute-start | bytes 1179656 | tf_op jit(solution)/shard_map/ppermute | solution.py:25
  (89 other events, 1084.9 us)
Sparse Core Ops, SparseCore 0:
  22.8 59.9 all-gather.2
  230.8 43.8 all-gather.4
  324.5 167.9 all-reduce.2
